TPU v7x, 512 devices: a whole 4x8x8 slice. The times are simulated.
512 devices in a mesh: expert: 64 (over x, z_lo, y), tensor: 8 (over z_hi, core).
Axes of the slice: x: 4, y: 8, z: 8 (z_hi: 4, z_lo: 2; z = z_hi * 2 + z_lo), core: 2. Of those that a mesh axis runs over, the one named last changes fastest.
Arguments:
- tokens: bfloat16 [16384, 3584], P('expert', 'tensor'), may hold values from -6 to 6
- expert_ids: int32 [16384, 2], P('expert'), may hold values from 0 to 63, all different within a row; in each aligned block of 256 rows (0 to 255, 256 to 511, ...) at most 12 rows name the same one
- weights: bfloat16 [64, 3584, 2, 2432], P('expert', None, None, 'tensor'), may hold values from -0.09375 to 0.09375
Outputs:
- hidden: bfloat16 [16384, 2, 2432], P('expert', None, 'tensor')
Inputs may be any that keep to these rules, and one draw needn't show every extreme that they name: `expert_ids`: the two experts of a token differ. Among the 256 tokens of one index of expert, at most 12 name any one expert, and that bound is reached.
All inputs are finite; a program needn't handle non-finite values.
Results may differ from a plain program's by a relative error of at most 0.0013.
Values may be sent and summed in bfloat16 or wider, within the bound.
A program may use at most 64 MiB of HBM per device.

v0:
```python
import jax
import jax.numpy as jnp
from jax import lax
from jax.sharding import PartitionSpec as P


def shards(tokens, expert_ids, weights):
    groups = lax.axis_size("expert")
    tok_rows = expert_ids.shape[0]
    capacity = 3 * tok_rows // groups
    routed = tok_rows * 2
    slots = groups * capacity
    flat_ids = expert_ids.reshape(routed)
    onehot = (flat_ids[:, None] == jnp.arange(groups, dtype=jnp.int32)[None, :]).astype(jnp.float32)
    row_iota = jnp.arange(routed, dtype=jnp.int32)
    lower = (row_iota[:, None] > row_iota[None, :]).astype(jnp.float32)
    before = jnp.dot(lower, onehot, precision=lax.Precision.HIGHEST)
    position = jnp.sum(before * onehot, axis=1).astype(jnp.int32)
    slot_of = flat_ids * capacity + position
    dispatch_map = (slot_of[None, :] == jnp.arange(slots, dtype=jnp.int32)[:, None]).astype(
        jnp.bfloat16
    )
    local_w = weights.reshape(weights.shape[1], 2 * weights.shape[3])
    width = weights.shape[3]
    doubled = jnp.repeat(tokens, 2, axis=0)
    outgoing = jnp.dot(dispatch_map, doubled, preferred_element_type=jnp.float32).astype(
        jnp.bfloat16
    )
    outgoing = outgoing.reshape(groups, capacity, tokens.shape[1])
    received = lax.all_to_all(outgoing, "expert", split_axis=0, concat_axis=0, tiled=True)
    flat_rows = received.reshape(-1, received.shape[2])
    gate_up = jnp.dot(
        lax.all_gather(flat_rows, "tensor", axis=1, tiled=True),
        local_w,
        preferred_element_type=jnp.float32,
    )
    received_shape = received.shape
    gate = gate_up[:, :width]
    up_part = gate_up[:, width:]
    hidden_rows = (jax.nn.silu(gate) * up_part).astype(jnp.bfloat16)
    hidden_rows = hidden_rows.reshape(received_shape[0], received_shape[1], width)
    returned = lax.all_to_all(hidden_rows, "expert", split_axis=0, concat_axis=0, tiled=True)
    flat_back = returned.reshape(slots, width)
    gathered = lax.dot_general(
        dispatch_map, flat_back, (((0,), (0,)), ((), ())), preferred_element_type=jnp.float32
    )
    return gathered.astype(jnp.bfloat16).reshape(tok_rows, 2, width)


def solution(mesh):
    return jax.shard_map(
        shards,
        mesh=mesh,
        in_specs=(P("expert", "tensor"), P("expert", None), P("expert", None, None, "tensor")),
        out_specs=P("expert", None, "tensor"),
        check_vma=False,
    )
```

profile of v0, /device:TPU:1, one launch (start us, length us, event | category | flops | bytes accessed | tf_op | source)
XLA Modules:
  0.0 169.5 jit_solution(8202005180666539561)
XLA Ops:
  6.5 0.8 copy.12
  7.4 0.1 reshape.34
  7.5 0.3 fusion.4
  7.8 1.1 copy.13
  8.9 0.3 broadcast_in_dim.2
  9.2 0.4 reshape.35
  9.6 0.6 fusion.2
  10.2 0.3 copy.14
  10.5 0.3 reshape.36
  10.8 39.3 %all_to_all.10 = bf16[64,12,448]{2,1,0:T(8,128)(2,1)S(1)} all-to-all(bf16[64,12,448]{2,1,0:T(8,128)(2,1)S(1)} %reshape.36), channel_id=1, replica_groups=mesh['expert'=64,'tensor'=8] {'expert'}, dimensions={0} | all-to-all | bytes 1376256 | tf_op jit(solution)/shard_map/all_to_all | solution.py:30
  50.0 0.4 reshape.37
  50.4 1.1 copy.15
  51.6 0.0 all-gather.2.cloned.1.call-update
  51.6 69.6 %all-gather.2.cloned.1.call-done = bf16[768,3584]{0,1:T(8,128)(2,1)} async-done(((bf16[768,448]{0,1:T(8,128)(2,1)}), bf16[768,3584]{0,1:T(8,128)(2,1)}) %all-gather.2.cloned.1.call-update) | async-done | bytes 5505040 | tf_op jit(solution)/shard_map/all_gather | solution.py:33
  121.2 6.9 %fusion.9 = f32[768,608]{0,1:T(8,128)S(1)} fusion(bf16[3584,608]{0,1:T(8,128)(2,1)} %bitcast.5, bf16[768,3584]{0,1:T(8,128)(2,1)} %all-gather.2.cloned.1.call-done), kind=kOutput, calls=%fused_computation.15 | convolution fusion | flops 3347054592 | bytes 11730944 | tf_op jit(solution)/shard_map/dot_general | solution.py:32
  128.1 0.3 fusion.5
  128.4 0.3 copy.16
  128.7 0.2 reshape.39
  128.9 31.4 %all_to_all.11 = bf16[64,12,304]{2,1,0:T(8,128)(2,1)S(1)} all-to-all(bf16[64,12,304]{2,1,0:T(8,128)(2,1)S(1)} %reshape.39), channel_id=1, replica_groups=mesh['expert'=64,'tensor'=8] {'expert'}, dimensions={0} | all-to-all | bytes 933888 | tf_op jit(solution)/shard_map/all_to_all | solution.py:42
  160.3 0.3 reshape.40
  160.6 0.5 fusion.3
  161.2 0.2 copy.17
  161.4 0.2 reshape.41
  161.6 1.1 copy.18
  (2 shorter events, 0.0 us)
Async XLA Ops:
  6.5 114.6 %all-gather.2.cloned.1.call-start = ((), (), s32[]{:S(2)}) async-start(), calls=%async_computation.2 | async-start | bytes 6193152 | tf_op jit(solution)/shard_map/all_gather | solution.py:33
Sparse Core Ops, SparseCore 0:
  51.7 69.3 all-gather.1
where the time goes:
time: 171 us; the launch traced here: 169 us
  blocking collectives  70.7 us (41%)
  waiting for transfers between devices  69.6 us (41%)
  between operations  13.5 us (8%)
  matrix products  8.36 us (5%)
  local copies, waits for them, and re-layouts  7.04 us (4%)
    all_gather x1, waiting for transfers between devices, shards(): lax.all_gather(flat_rows, 'tensor', axis=1, tiled=True)  69.6 us
    all_to_all x1, blocking collectives, shards(): lax.all_to_all(outgoing, 'expert', split_axis=0, concat_axis=0, tiled=True)  39.3 us
    all_to_all x1, blocking collectives, shards(): lax.all_to_all(hidden_rows, 'expert', split_axis=0, concat_axis=0, tiled=...  31.4 us
    dot_general x1, matrix products, shards(): jnp.dot(lax.all_gather(flat_rows, 'tensor', axis=1, tiled=True), local_w,...  6.95 us
  transfers between devices with their start and end apart: 1, of which 1 were waited for; matrix products, arithmetic and copies ran while one was open for 0% of the time, Pallas kernels for 0%

commit v1 on v0

v1 whole, which is shorter than its diff:
```python
import functools

import jax
import jax.numpy as jnp
from jax import lax
from jax.experimental import pallas as pl
from jax.experimental.pallas import tpu as pltpu
from jax.sharding import PartitionSpec as P

MESH = pl.DeviceIdType.MESH
BF = jnp.bfloat16
F32 = jnp.float32

GROUPS = 3
LANES = 896
HALF = 448
WIDTH = 304
RET = 640
OUTW = 384
UNITS = [(0, 0, 384), (0, 384, 512), (1, 0, 384), (1, 384, 512), (2, 0, 512), (2, 512, 384)]
LAST = {0: 1, 1: 3, 2: 5}


def dot(a, b, dims):
    return lax.dot_general(a, b, (dims, ((), ())), preferred_element_type=F32)


def kernel(
    ids_ref, tok_ref, w_ref, out_ref,
    tokt, ww, ysend, yrecv, xsend, fs, xf, acc, hb, rx, rys, ry, rd, gmap, oacc,
    tsem, wsem, csem, ysem, xsem, zsend, zrecv, r1sem, r2sem, r3sem,
):
    e = lax.axis_index("expert")
    t = lax.axis_index("tensor")
    y = lax.rem(e, 8)
    q = e // 8
    x = q // 2
    zl = lax.rem(q, 2)
    h = t // 2
    c = lax.rem(t, 2)

    def dev(x_, zl_, y_, h_):
        return ((x_ * 2 + zl_) * 8 + y_, h_ * 2 + c)

    other = (e, h * 2 + 1 - c)
    zp1 = dev(x, 1 - zl, y, lax.rem(h + zl, 4))
    zm1 = dev(x, 1 - zl, y, lax.rem(h + zl + 3, 4))
    zp2 = dev(x, zl, y, lax.rem(h + 1, 4))
    zm2 = dev(x, zl, y, lax.rem(h + 3, 4))
    ypeers = [(lax.rem(y + d, 8), dev(x, zl, lax.rem(y + d, 8), h)) for d in (4, 3, 5, 2, 6, 1, 7)]
    xpeers = [(lax.rem(x + d, 4), dev(lax.rem(x + d, 4), zl, y, h)) for d in (2, 1, 3)]
    qpeers = [
        (lax.rem(x + d, 4), f, dev(lax.rem(x + d, 4), (1 - zl) if f else zl, y, h))
        for d, f in ((2, 1), (1, 1), (3, 1), (2, 0), (1, 0), (3, 0), (0, 1))
    ]

    barrier = pltpu.get_barrier_semaphore()
    peers = [p for _, p in ypeers] + [p for _, _, p in qpeers] + [zp1, zm1, zp2, zm2, other]
    for p in peers:
        pl.semaphore_signal(barrier, inc=1, device_id=p, device_id_type=MESH)

    def remote(src, dst, ss, rs, p):
        return pltpu.make_async_remote_copy(
            src_ref=src, dst_ref=dst, send_sem=ss, recv_sem=rs, device_id=p, device_id_type=MESH
        )

    mine = pl.ds(pl.multiple_of(c * HALF, 16), HALF)
    theirs = pl.ds(pl.multiple_of((1 - c) * HALF, 16), HALF)
    tok_local = pltpu.make_async_copy(tok_ref, tokt.at[mine], tsem.at[0])
    tok_local.start()
    w_local = pltpu.make_async_copy(w_ref, ww.at[c], wsem.at[0])
    w_local.start()

    experts = lax.broadcasted_iota(jnp.int32, (64, 256), 0)
    upper = (
        lax.broadcasted_iota(jnp.int32, (256, 256), 0) < lax.broadcasted_iota(jnp.int32, (256, 256), 1)
    ).astype(F32).astype(BF)
    counted = jnp.zeros((64, 1), F32)
    slots = []
    for k in range(2):
        expert = ids_ref[k : k + 1, :]
        hot = (experts == expert).astype(F32)
        before = dot(hot.astype(BF), upper, ((1,), (0,))) + counted
        counted = counted + jnp.sum(hot, axis=1, keepdims=True)
        rank = jnp.sum(before * hot, axis=0, keepdims=True).astype(jnp.int32)
        ey, eq = expert & 7, expert >> 3
        flip = (eq + zl) & 1
        row = ey * 16 + (eq >> 1) * 4 + flip * 2 + ((rank >> 1) & 1)
        slots.append(((rank & 1) * GROUPS + (rank >> 2)) * 128 + row)
    rows_iota = lax.broadcasted_iota(jnp.int32, (128, 256), 0)

    def build_map(n, i):
        for k in range(2):
            gmap[n, :, k * 256 : (k + 1) * 256] = (slots[k] == rows_iota + i * 128).astype(F32).astype(BF)

    r_out = lax.broadcasted_iota(jnp.int32, (128, 128), 0)
    r_in = lax.broadcasted_iota(jnp.int32, (128, 128), 1)
    perm = (r_in == (r_out & 15) // 2 * 16 + (r_out >> 4) * 2 + (r_out & 1)).astype(F32).astype(BF)

    for g in range(GROUPS):
        build_map(g, c * GROUPS + g)

    pl.semaphore_wait(barrier, len(peers))
    tok_local.wait()
    tok_remote = remote(tokt.at[mine], tokt.at[mine], tsem.at[1], tsem.at[2], other)
    tok_remote.start()
    w_remote = remote(w_ref, ww.at[c], wsem.at[1], wsem.at[2], other)
    w_remote.start()
    for g in range(GROUPS):
        build_map(GROUPS + g, (1 - c) * GROUPS + g)
    remote(tokt.at[mine], tokt.at[theirs], tsem.at[1], tsem.at[2], other).wait_recv()

    def stage_a(u):
        g, f, n = UNITS[u]
        part = pl.ds(f, n)
        dispatch = gmap[g, :, :256] + gmap[g, :, 256:]
        rows = dot(dispatch, tokt[f : f + n, :], ((1,), (1,))).astype(BF)
        ysend[g, :, :, part] = rows.reshape(8, 16, n)
        for j, p in ypeers:
            remote(ysend.at[g, j, :, part], yrecv.at[g, y, :, part], ysem.at[0, u], ysem.at[1, u], p).start()
        yrecv[g, y, :, part] = ysend[g, y, :, part]

    def y_done(u):
        g, f, n = UNITS[u]
        part = pl.ds(f, n)
        return remote(
            ysend.at[g, pl.ds(0, 7), :, part], yrecv.at[g, pl.ds(0, 7), :, part], ysem.at[0, u], ysem.at[1, u], other
        )

    def stage_b(u):
        g, f, n = UNITS[u]
        part = pl.ds(f, n)
        y_done(u).wait_recv()
        rows = yrecv[g, :, :, part].reshape(128, n)
        xsend[g, :, :, :, part] = dot(perm, rows, ((1,), (0,))).astype(BF).reshape(4, 2, 16, n)
        for j, p in xpeers:
            remote(xsend.at[g, j, 0, :, part], xf.at[g, h, 0, x, :, part], xsem.at[0, u], xsem.at[1, u], p).start()
            remote(xsend.at[g, j, 1, :, part], fs.at[g, x, :, part], xsem.at[2, u], xsem.at[3, u], p).start()
        xf[g, h, 0, x, :, part] = xsend[g, x, 0, :, part]
        fs[g, x, :, part] = xsend[g, x, 1, :, part]

    def x_done(u, k):
        g, f, n = UNITS[u]
        part = pl.ds(f, n)
        three = fs.at[g, pl.ds(0, 3), :, part]
        return remote(three, three, xsem.at[2 * k, u], xsem.at[2 * k + 1, u], other)

    def z_copies(u):
        g, f, n = UNITS[u]
        part = pl.ds(f, n)

        def near(o):
            return xf.at[g, o, 0, :, :, part]

        def half(o, k):
            return xf.at[g, o, 0, pl.ds(2 * k, 2), :, part]

        def far(o):
            return xf.at[g, o, 1, :, :, part]

        mod = lambda v: lax.rem(v, 4)
        out = [
            (near(h), near(h), zp2), (near(h), near(h), zm2),
            (fs.at[g, :, :, part], far(h), zp1), (fs.at[g, :, :, part], far(h), zm1),
            (half(mod(h + 3), 0), half(mod(h + 3), 0), zp2), (half(mod(h + 1), 1), half(mod(h + 1), 1), zm2),
            (far(mod(h + zl + 3)), far(mod(h + zl + 3)), zp2), (far(mod(h + zl)), far(mod(h + zl)), zm2),
        ]
        inn = [
            near(mod(h + 3)), near(mod(h + 1)), far(mod(h + zl + 3)), far(mod(h + zl)),
            half(mod(h + 2), 0), half(mod(h + 2), 1), far(mod(h + zl + 2)), far(mod(h + zl + 1)),
        ]
        return (
            lambda k: remote(out[k][0], out[k][1], zsend.at[k, u], zrecv.at[k, u], out[k][2]),
            lambda k: remote(inn[k], inn[k], zsend.at[k, u], zrecv.at[k, u], other),
        )

    def stage_c(u):
        out, _ = z_copies(u)
        x_done(u, 1).wait_recv()
        out(2).start()
        out(3).start()
        x_done(u, 0).wait_recv()
        out(0).start()
        out(1).start()

    def stage_d(u):
        out, inn = z_copies(u)
        for k, m in ((2, 6), (3, 7), (0, 4), (1, 5)):
            inn(k).wait_recv()
            out(m).start()

    def stage_e(u):
        g, f, n = UNITS[u]
        _, inn = z_copies(u)
        for k in (6, 7, 4, 5):
            inn(k).wait_recv()
        if f == 0:
            acc[...] = jnp.zeros_like(acc)

        def origin(o, carry):
            rows = xf[g, o, :, :, :, pl.ds(f, n)].reshape(128, n)
            cols = pl.ds(pl.multiple_of(o * LANES + f, 128), n)
            for j in range(2):
                acc[j] += dot(rows, ww[j, :, cols], ((1,), (1,)))
            return carry

        lax.fori_loop(0, 4, origin, 0)

    def stage_r1(g):
        for j in range(2):
            gate, up = acc[j, :, :WIDTH], acc[j, :, WIDTH:]
            value = (gate / (1.0 + jnp.exp(-gate)) * up).astype(BF)
            hb[g, :, :, :, j * WIDTH : (j + 1) * WIDTH] = value.reshape(2, 4, 16, WIDTH)
        for j, fl, p in qpeers:
            remote(hb.at[g, fl, j], rx.at[g, x, fl], r1sem.at[0, g], r1sem.at[1, g], p).start()
        rx[g, x, 0] = hb[g, 0, x]

    def r1_done(g):
        seven = ry.at[g, pl.ds(0, 7)]
        return remote(seven, seven, r1sem.at[0, g], r1sem.at[1, g], other)

    def stage_r2(g):
        r1_done(g).wait_recv()
        rows = rx[g].reshape(128, RET)
        rys[g] = dot(perm, rows, ((1,), (0,))).astype(BF).reshape(8, 16, RET)
        for j, p in ypeers:
            remote(rys.at[g, j], ry.at[g, y], r2sem.at[0, g], r2sem.at[1, g], p).start()
        ry[g, y] = rys[g, y]

    def r2_done(g):
        seven = ry.at[g, pl.ds(0, 7)]
        return remote(seven, seven, r2sem.at[0, g], r2sem.at[1, g], other)

    def r3_copy(g):
        cols = pl.ds(pl.multiple_of((1 - c) * 256, 128), OUTW)
        return remote(ry.at[g, :, :, cols], rd.at[g], r3sem.at[0, g], r3sem.at[1, g], other)

    def stage_r3(g):
        r2_done(g).wait_recv()
        r3_copy(g).start()
        own = ry[g, :, :, pl.ds(pl.multiple_of(c * 256, 128), OUTW)].reshape(128, OUTW)
        part = dot(own, gmap[g], ((0,), (0,)))
        oacc[...] = part if g == 0 else oacc[...] + part

    def stage_r4(g):
        r3_copy(g).wait_recv()
        oacc[...] += dot(rd[g].reshape(128, OUTW), gmap[GROUPS + g], ((0,), (0,)))

    hb[...] = jnp.zeros_like(hb)
    stage_a(0)
    stage_a(1)
    stage_b(0)
    stage_a(2)
    stage_c(0)
    stage_b(1)
    stage_a(3)
    stage_c(1)
    stage_b(2)
    stage_a(4)
    stage_d(0)
    stage_c(2)
    stage_b(3)
    stage_a(5)
    w_local.wait()
    w_remote.wait()
    stage_d(1)
    stage_c(3)
    stage_e(0)
    stage_b(4)
    stage_d(2)
    stage_c(4)
    stage_e(1)
    stage_r1(0)
    stage_b(5)
    stage_d(3)
    stage_c(5)
    stage_r2(0)
    stage_e(2)
    stage_d(4)
    stage_r3(0)
    stage_e(3)
    stage_r1(1)
    stage_d(5)
    stage_r4(0)
    stage_e(4)
    stage_r2(1)
    stage_e(5)
    stage_r1(2)
    stage_r3(1)
    stage_r4(1)
    stage_r2(2)
    stage_r3(2)
    stage_r4(2)
    start = pl.multiple_of(c * 48, 16)
    for k in range(2):
        out_ref[k] = oacc[pl.ds(start, WIDTH), k * 256 : (k + 1) * 256].astype(BF)

    tok_remote.wait_send()
    for u in range(len(UNITS)):
        y_done(u).wait_send()
        x_done(u, 0).wait_send()
        x_done(u, 1).wait_send()
        for k in range(8):
            z_copies(u)[0](k).wait_send()
    for g in range(GROUPS):
        r1_done(g).wait_send()
        r2_done(g).wait_send()
        r3_copy(g).wait_send()


def shards(tokens, expert_ids, weights):
    tok = tokens.T
    ids = expert_ids.T
    w = weights.transpose(0, 2, 3, 1).reshape(2 * WIDTH, weights.shape[1])
    units = len(UNITS)
    vmem = pltpu.VMEM
    dma = pltpu.SemaphoreType.DMA
    out = pl.pallas_call(
        kernel,
        out_shape=jax.ShapeDtypeStruct((2, WIDTH, 256), BF),
        in_specs=[
            pl.BlockSpec(memory_space=pltpu.VMEM),
            pl.BlockSpec(memory_space=pl.ANY),
            pl.BlockSpec(memory_space=pl.ANY),
        ],
        out_specs=pl.BlockSpec(memory_space=pltpu.VMEM),
        scratch_shapes=[
            vmem((LANES, 256), BF),
            vmem((2, 2 * WIDTH, 3584), BF),
            vmem((GROUPS, 8, 16, LANES), BF),
            vmem((GROUPS, 8, 16, LANES), BF),
            vmem((GROUPS, 4, 2, 16, LANES), BF),
            vmem((GROUPS, 4, 16, LANES), BF),
            vmem((GROUPS, 4, 2, 4, 16, LANES), BF),
            vmem((2, 128, 2 * WIDTH), F32),
            vmem((GROUPS, 2, 4, 16, RET), BF),
            vmem((GROUPS, 4, 2, 16, RET), BF),
            vmem((GROUPS, 8, 16, RET), BF),
            vmem((GROUPS, 8, 16, RET), BF),
            vmem((GROUPS, 8, 16, OUTW), BF),
            vmem((2 * GROUPS, 128, 512), BF),
            vmem((OUTW, 512), F32),
            dma((3,)),
            dma((3,)),
            dma((1,)),
            dma((2, units)),
            dma((4, units)),
            dma((8, units)),
            dma((8, units)),
            dma((2, GROUPS)),
            dma((2, GROUPS)),
            dma((2, GROUPS)),
        ],
        compiler_params=pltpu.CompilerParams(
            collective_id=1, has_side_effects=True, vmem_limit_bytes=56 << 20
        ),
        cost_estimate=pl.CostEstimate(flops=3355443200, bytes_accessed=5000000, transcendentals=233472),
        name="routed_projections",
    )(ids, tok, w)
    return out.transpose(2, 0, 1)


def solution(mesh):
    return jax.shard_map(
        shards,
        mesh=mesh,
        in_specs=(P("expert", "tensor"), P("expert", None), P("expert", None, None, "tensor")),
        out_specs=P("expert", None, "tensor"),
        check_vma=False,
    )
```

time: 171 us -> 95.5 us (0.56)
  Pallas kernels: 0 us -> 93.7 us
  blocking collectives: 70.7 us -> 0 us
  waiting for transfers between devices: 69.6 us -> 0 us
  between operations: 13.5 us -> 0.01 us
  matrix products: 8.36 us -> 0 us
  local copies, waits for them, and re-layouts: 7.04 us -> 1.71 us
    pallas_call x0 -> x1, Pallas kernels: none -> 93.7 us  [shards(): pl.pallas_call(kernel, out_shape=jax.ShapeDtypeStruct((2, WIDTH, 256), BF...]
    all_to_all x2 -> x0, blocking collectives: 70.7 us -> none  [the longest x1 39.3 us: shards(): lax.all_to_all(outgoing, 'expert', split_axis=0, concat_axis=0, tiled=True)]
    all_gather x1 -> x0, waiting for transfers between devices: 69.6 us -> none  [shards(): lax.all_gather(flat_rows, 'tensor', axis=1, tiled=True)]
    dot_general x4 -> x0, matrix products: 8.36 us -> none  [the longest x1 6.95 us: shards(): jnp.dot(lax.all_gather(flat_rows, 'tensor', axis=1, tiled=True), local_w,...]
    reshape x9 -> x0, local copies, waits for them, and re-layouts: 4.1 us -> none  [the longest x2 1.54 us: shards(): flat_rows = received.reshape(-1, received.shape[2])]
  transfers between devices with their start and end apart: 1 -> 0, of which waited for: 1 -> 0; matrix products, arithmetic and copies ran while one was open for 0% -> 0% of each run, Pallas kernels for 0% -> 0%
where the time goes in v1:
time: 95.5 us; the launch traced here: 95.4 us
  Pallas kernels  93.7 us (98%)
  local copies, waits for them, and re-layouts  1.71 us (2%)
    pallas_call x1, Pallas kernels, shards(): pl.pallas_call(kernel, out_shape=jax.ShapeDtypeStruct((2, WIDTH, 256), BF...  93.7 us

profile of v1, /device:TPU:1, one launch (start us, length us, event | category | flops | bytes accessed | tf_op | source)
XLA Modules:
  0.0 95.4 jit_solution(18112032071148655493)
XLA Ops:
  0.0 93.7 %routed_projections.1 = bf16[2,304,256]{2,1,0:T(8,128)(2,1)} custom-call(s32[2,256]{1,0:T(2,128)} %bitcast.9, bf16[448,256]{1,0:T(8,128)(2,1)} %bitcast.8, bf16[608,3584]{1,0:T(8,128)(2,1)} %bitcast.7), custom_call_target="tpu_custom_call" | custom-call | flops 3355443200 | bytes 5000000 | tf_op jit(solution)/shard_map/routed_projections/pallas_call | solution.py:318
  93.7 1.7 %copy.5 = bf16[256,2,304]{0,2,1:T(8,128)(2,1)} copy(bf16[256,2,304]{0,2,1:T(8,128)(2,1)} %bitcast.6) | data formatting | bytes 622592

commit v2 on v1

v2 whole, which is shorter than its diff:
```python
import functools

import jax
import jax.numpy as jnp
from jax import lax
from jax.experimental import pallas as pl
from jax.experimental.pallas import tpu as pltpu
from jax.sharding import PartitionSpec as P

MESH = pl.DeviceIdType.MESH
BF = jnp.bfloat16
F32 = jnp.float32

GROUPS = 3
HALF = 448
AW = 384
BW = 512
BF_ROWS = 64
WIDTH = 304
RET = 384
UNITS = [(0, 0), (0, 1), (1, 0), (1, 1), (2, 0), (2, 1)]


def dot(a, b, dims):
    return lax.dot_general(a, b, (dims, ((), ())), preferred_element_type=F32)


def kernel(
    ids_ref, tok_ref, w_ref, out_ref,
    tokm, toko, tb, ido, ww, ysend, yrecv, xsend, fs, xf, ysb, yrb, xsb, xb,
    acc, hb, rx, rys, rd, gmap, bmap, oacc,
    tsem, wsem, bsem, ysem, xsem, zsend, zrecv, ybsem, xbsem, r1sem, r2sem,
):
    e = lax.axis_index("expert")
    t = lax.axis_index("tensor")
    y = lax.rem(e, 8)
    q = e // 8
    x = q // 2
    zl = lax.rem(q, 2)
    h = t // 2
    c = lax.rem(t, 2)

    def dev(x_, zl_, y_, h_):
        return ((x_ * 2 + zl_) * 8 + y_, h_ * 2 + c)

    def mod4(v):
        return lax.rem(v, 4)

    def across(d):
        return (d[0], d[1] + 1 - 2 * c)

    other = across((e, t))
    zp1 = dev(x, 1 - zl, y, mod4(h + zl))
    zm1 = dev(x, 1 - zl, y, mod4(h + zl + 3))
    zp2 = dev(x, zl, y, mod4(h + 1))
    zm2 = dev(x, zl, y, mod4(h + 3))
    zp3 = dev(x, 1 - zl, y, mod4(h + zl + 1))
    zm3 = dev(x, 1 - zl, y, mod4(h + zl + 2))
    zp4 = dev(x, zl, y, mod4(h + 2))
    line = [zp1, zm1, zp2, zm2, zp3, zm3, zp4]
    ypeers = [(lax.rem(y + d, 8), dev(x, zl, lax.rem(y + d, 8), h)) for d in (4, 3, 5, 2, 6, 1, 7)]
    xpeers = [(mod4(x + d), dev(mod4(x + d), zl, y, h)) for d in (2, 1, 3)]
    qpeers = [
        (mod4(x + d), f, dev(mod4(x + d), (1 - zl) if f else zl, y, h))
        for d, f in ((2, 1), (1, 1), (3, 1), (2, 0), (1, 0), (3, 0), (0, 1))
    ]
    twin = dev(x, 1 - zl, y, h)

    barrier = pltpu.get_barrier_semaphore()
    peers = [p for _, p in ypeers] + [across(p) for _, p in ypeers] + [p for _, _, p in qpeers] + line + [other]
    for p in peers:
        pl.semaphore_signal(barrier, inc=1, device_id=p, device_id_type=MESH)

    def remote(src, dst, ss, rs, p):
        return pltpu.make_async_remote_copy(
            src_ref=src, dst_ref=dst, send_sem=ss, recv_sem=rs, device_id=p, device_id_type=MESH
        )

    tok_local = pltpu.make_async_copy(tok_ref, tokm, tsem.at[0])
    tok_local.start()
    w_local = pltpu.make_async_copy(w_ref, ww.at[0], wsem.at[0])
    w_local.start()

    experts = lax.broadcasted_iota(jnp.int32, (64, 256), 0)
    upper = (
        lax.broadcasted_iota(jnp.int32, (256, 256), 0) < lax.broadcasted_iota(jnp.int32, (256, 256), 1)
    ).astype(F32).astype(BF)

    def slots_of(ids, source_zl):
        counted = jnp.zeros((64, 1), F32)
        slots = []
        for k in range(2):
            expert = ids[k : k + 1, :]
            hot = (experts == expert).astype(F32)
            before = dot(hot.astype(BF), upper, ((1,), (0,))) + counted
            counted = counted + jnp.sum(hot, axis=1, keepdims=True)
            rank = jnp.sum(before * hot, axis=0, keepdims=True).astype(jnp.int32)
            ey, eq = expert & 7, expert >> 3
            flip = (eq + source_zl) & 1
            row = ey * 16 + (eq >> 1) * 4 + flip * 2 + ((rank >> 1) & 1)
            slots.append(((rank & 1) * GROUPS + (rank >> 2)) * 128 + row)
        return slots

    rows_iota = lax.broadcasted_iota(jnp.int32, (128, 256), 0)
    slots = slots_of(ids_ref, zl)

    def build_map(g, k):
        wanted = rows_iota + ((c if k == 0 else 1 - c) * GROUPS + g) * 128
        for choice in range(2):
            gmap[g, k, :, choice * 256 : (choice + 1) * 256] = (slots[choice] == wanted).astype(F32).astype(BF)

    r_out = lax.broadcasted_iota(jnp.int32, (128, 128), 0)
    r_in = lax.broadcasted_iota(jnp.int32, (128, 128), 1)
    perm = (r_in == (r_out & 15) // 2 * 16 + (r_out >> 4) * 2 + (r_out & 1)).astype(F32).astype(BF)

    build_map(0, 0)

    b_rows = pl.ds(pl.multiple_of((1 - c) * AW, 16), BF_ROWS)
    b_dst = pl.ds(pl.multiple_of(c * BF_ROWS, 16), BF_ROWS)
    a_rows = pl.ds(pl.multiple_of(c * BF_ROWS, 16), AW)

    tok_local.wait()
    pl.semaphore_wait(barrier, len(peers))
    tok_remote = remote(tokm.at[a_rows], toko, tsem.at[1], tsem.at[2], other)
    tok_remote.start()
    ids_remote = remote(ids_ref, ido, bsem.at[0], bsem.at[1], twin)
    ids_remote.start()

    def stage_s(_):
        for p in line:
            remote(tokm.at[b_rows], tb.at[zl, h, b_dst], bsem.at[2], bsem.at[3], p).start()
        tb[zl, h, b_dst] = tokm[b_rows]

    def s_done():
        n = BF_ROWS * 7
        return remote(tokm.at[pl.ds(0, n)], tokm.at[pl.ds(0, n)], bsem.at[2], bsem.at[3], other)

    def pass_copy():
        return remote(tb.at[:, :, b_dst], tb.at[:, :, b_dst], bsem.at[4], bsem.at[5], other)

    def stage_t(_):
        s_done().wait_recv()
        pass_copy().start()

    def stage_m(k):
        for g in range(1 - k, GROUPS):
            build_map(g, k)

    def stage_n(_):
        ids_remote.wait_recv()
        theirs = slots_of(ido, 1 - zl)
        flips = (rows_iota >> 1) & 1
        for g in range(GROUPS):
            wanted = rows_iota + (c * GROUPS + g) * 128
            here = (gmap[g, 0, :, :256] + gmap[g, 0, :, 256:]).astype(F32)
            there = jnp.where((theirs[0] == wanted) | (theirs[1] == wanted), 1.0, 0.0)
            bmap[g, :, :256] = jnp.where(flips == 0, here, 0.0).astype(BF)
            bmap[g, :, 256:] = jnp.where(flips == 1, there, 0.0).astype(BF)

    def stage_a(u):
        g, p = UNITS[u]
        dispatch = gmap[g, 0, :, :256] + gmap[g, 0, :, 256:]
        if u == 1:
            remote(toko, toko, tsem.at[1], tsem.at[2], other).wait_recv()
        features = tokm[a_rows] if p == 0 else toko[...]
        ysend[p, g] = dot(dispatch, features, ((1,), (1,))).astype(BF).reshape(8, 16, AW)
        for j, d in ypeers:
            remote(ysend.at[p, g, j], yrecv.at[p, g, y], ysem.at[0, u], ysem.at[1, u], d).start()
        yrecv[p, g, y] = ysend[p, g, y]

    def y_done(u):
        g, p = UNITS[u]
        seven = yrecv.at[p, g, pl.ds(0, 7)]
        return remote(seven, seven, ysem.at[0, u], ysem.at[1, u], other)

    def stage_b(u):
        g, p = UNITS[u]
        y_done(u).wait_recv()
        rows = yrecv[p, g].reshape(128, AW)
        xsend[p, g] = dot(perm, rows, ((1,), (0,))).astype(BF).reshape(4, 2, 16, AW)
        for j, d in xpeers:
            remote(xsend.at[p, g, j, 1], fs.at[p, g, x], xsem.at[2, u], xsem.at[3, u], d).start()
        for j, d in xpeers:
            remote(xsend.at[p, g, j, 0], xf.at[p, g, h, 0, x], xsem.at[0, u], xsem.at[1, u], d).start()
        xf[p, g, h, 0, x] = xsend[p, g, x, 0]
        fs[p, g, x] = xsend[p, g, x, 1]

    def x_done(u, k):
        g, p = UNITS[u]
        three = fs.at[p, g, pl.ds(0, 3)]
        return remote(three, three, xsem.at[2 * k, u], xsem.at[2 * k + 1, u], other)

    def z_copies(u):
        g, p = UNITS[u]

        def near(o):
            return xf.at[p, g, o, 0]

        def half(o, k):
            return xf.at[p, g, o, 0, pl.ds(2 * k, 2)]

        def far(o):
            return xf.at[p, g, o, 1]

        out = [
            (near(h), near(h), zp2), (near(h), near(h), zm2),
            (fs.at[p, g], far(h), zp1), (fs.at[p, g], far(h), zm1),
            (half(mod4(h + 3), 0), half(mod4(h + 3), 0), zp2), (half(mod4(h + 1), 1), half(mod4(h + 1), 1), zm2),
            (far(mod4(h + zl + 3)), far(mod4(h + zl + 3)), zp2), (far(mod4(h + zl)), far(mod4(h + zl)), zm2),
        ]
        inn = [
            near(mod4(h + 3)), near(mod4(h + 1)), far(mod4(h + zl + 3)), far(mod4(h + zl)),
            half(mod4(h + 2), 0), half(mod4(h + 2), 1), far(mod4(h + zl + 2)), far(mod4(h + zl + 1)),
        ]
        return (
            lambda k: remote(out[k][0], out[k][1], zsend.at[k, u], zrecv.at[k, u], out[k][2]),
            lambda k: remote(inn[k], inn[k], zsend.at[k, u], zrecv.at[k, u], other),
        )

    def stage_c(u):
        out, _ = z_copies(u)
        x_done(u, 1).wait_recv()
        out(2).start()
        out(3).start()
        x_done(u, 0).wait_recv()
        out(0).start()
        out(1).start()

    def stage_d(u):
        out, inn = z_copies(u)
        for k, m in ((2, 6), (3, 7), (0, 4), (1, 5)):
            inn(k).wait_recv()
            out(m).start()

    def stage_e(u):
        stage_w(u)
        for k in range(2):
            stage_f(u, k)

    def stage_w(u):
        _, inn = z_copies(u)
        for k in (6, 7, 4, 5):
            inn(k).wait_recv()

    def stage_f(u, k):
        g, p = UNITS[u]
        first = (c if p == 0 else 1 - c) * BW
        total = jnp.zeros((2 * WIDTH, 128), F32) if p == 0 else acc[k]
        for o in range(4):
            cols = pl.ds(pl.multiple_of(o * 2 * HALF + first, 128), AW)
            total = total + dot(ww[k, :, cols], xf[p, g, o].reshape(128, AW), ((1,), (1,)))
        acc[k] = total

    def stage_ab(g):
        if g == 0:
            pass_copy().wait_recv()
        rows = jnp.zeros((128, BW), F32)
        for s, plane in ((0, zl), (1, 1 - zl)):
            features = tb[plane].reshape(BW, 256)
            rows = rows + dot(bmap[g, :, s * 256 : (s + 1) * 256], features, ((1,), (1,)))
        ysb[g] = rows.astype(BF).reshape(8, 16, BW)
        for j, d in ypeers:
            remote(ysb.at[g, j], yrb.at[g, y], ybsem.at[0, g], ybsem.at[1, g], d).start()
        yrb[g, y] = ysb[g, y]

    def yb_done(g):
        seven = yrb.at[g, pl.ds(0, 7)]
        return remote(seven, seven, ybsem.at[0, g], ybsem.at[1, g], other)

    def stage_bb(g):
        yb_done(g).wait_recv()
        rows = yrb[g].reshape(128, BW)
        xsb[g] = dot(perm, rows, ((1,), (0,))).astype(BF).reshape(4, 2, 16, BW)
        for j, d in xpeers:
            remote(xsb.at[g, j], xb.at[g, x], xbsem.at[0, g], xbsem.at[1, g], d).start()
        xb[g, x] = xsb[g, x]

    def xb_done(g):
        three = xb.at[g, pl.ds(0, 3)]
        return remote(three, three, xbsem.at[0, g], xbsem.at[1, g], other)

    def stage_eb(g):
        xb_done(g).wait_recv()
        for k in range(2):
            total = acc[k]
            for o in range(4):
                lanes = slice(o * 128, (o + 1) * 128)
                rows = jnp.concatenate([xb[g, :, f, :, lanes].reshape(64, 128) for f in range(2)])
                cols = slice(o * 2 * HALF + AW, o * 2 * HALF + BW)
                total = total + dot(ww[k, :, cols], rows, ((1,), (1,)))
            acc[k] = total

    def stage_r1(g):
        for k in range(2):
            stage_h(g, k)

    def stage_h(g, k):
        gate, up = acc[k, :WIDTH, :], acc[k, WIDTH:, :]
        value = gate / (1.0 + jnp.exp(-gate)) * up
        value = jnp.concatenate([value, jnp.zeros((RET - WIDTH, 128), F32)])
        hb[k, g] = value.T.astype(BF).reshape(2, 4, 16, RET)
        for j, fl, p in qpeers:
            remote(hb.at[k, g, fl, j], rx.at[k, g, x, fl], r1sem.at[0, k, g], r1sem.at[1, k, g], p).start()
        rx[k, g, x, 0] = hb[k, g, 0, x]

    def r1_done(g, k):
        seven = rd.at[g, pl.ds(0, 7)]
        return remote(seven, seven, r1sem.at[0, k, g], r1sem.at[1, k, g], other)

    def stage_r2(g):
        for k in range(2):
            stage_k(g, k)

    def stage_k(g, k):
        r1_done(g, k).wait_recv()
        rows = rx[k, g].reshape(128, RET)
        rys[k, g] = dot(perm, rows, ((1,), (0,))).astype(BF).reshape(8, 16, RET)
        for j, p in ypeers:
            to = p if k == 0 else across(p)
            remote(rys.at[k, g, j], rd.at[g, k * 8 + y], r2sem.at[0, g], r2sem.at[1, g], to).start()
        if k == 0:
            rd[g, y] = rys[0, g, y]
        else:
            remote(rys.at[1, g, y], rd.at[g, 8 + y], r2sem.at[0, g], r2sem.at[1, g], other).start()

    def r2_done(g):
        fifteen = rd.at[g, pl.ds(0, 15)]
        return remote(fifteen, fifteen, r2sem.at[0, g], r2sem.at[1, g], other)

    def stage_r4(g):
        r2_done(g).wait_recv()
        part = dot(rd[g].reshape(256, RET), gmap[g].reshape(256, 512), ((0,), (0,)))
        oacc[...] = part if g == 0 else oacc[...] + part

    stage_a(0)
    stage_s(0)
    stage_m(0)
    stage_a(1)
    w_remote = remote(w_ref, ww.at[1], wsem.at[1], wsem.at[2], other)
    w_remote.start()
    stage_a(2)
    stage_b(0)
    stage_c(0)
    stage_a(3)
    stage_b(1)
    stage_c(1)
    stage_n(0)
    stage_a(4)
    stage_b(2)
    stage_d(0)
    stage_c(2)
    stage_a(5)
    stage_b(3)
    stage_t(0)
    stage_d(1)
    stage_c(3)
    stage_ab(0)
    stage_m(1)
    stage_b(4)
    stage_ab(1)
    w_local.wait()
    w_remote.wait()
    stage_e(0)
    stage_d(2)
    stage_c(4)
    stage_b(5)
    stage_ab(2)
    stage_bb(0)
    stage_e(1)
    stage_eb(0)
    stage_r1(0)
    stage_d(3)
    stage_c(5)
    stage_bb(1)
    stage_e(2)
    stage_d(4)
    stage_r2(0)
    stage_e(3)
    stage_eb(1)
    stage_r1(1)
    stage_bb(2)
    stage_d(5)
    stage_e(4)
    stage_eb(2)
    stage_r2(1)
    stage_r4(0)
    stage_w(5)
    stage_f(5, 0)
    stage_h(2, 0)
    stage_f(5, 1)
    stage_h(2, 1)
    stage_r4(1)
    stage_k(2, 0)
    stage_k(2, 1)
    stage_r4(2)
    for k in range(2):
        out_ref[k] = oacc[:WIDTH, k * 256 : (k + 1) * 256].astype(BF)

    tok_remote.wait_send()
    ids_remote.wait_send()
    s_done().wait_send()
    pass_copy().wait_send()
    for u in range(len(UNITS)):
        y_done(u).wait_send()
        x_done(u, 0).wait_send()
        x_done(u, 1).wait_send()
        for k in range(8):
            z_copies(u)[0](k).wait_send()
    for g in range(GROUPS):
        yb_done(g).wait_send()
        xb_done(g).wait_send()
        r1_done(g, 0).wait_send()
        r1_done(g, 1).wait_send()
        r2_done(g).wait_send()


def shards(tokens, expert_ids, weights):
    tok = tokens.T
    ids = expert_ids.T
    w = weights.transpose(0, 2, 3, 1).reshape(2 * WIDTH, weights.shape[1])
    units = len(UNITS)
    vmem = pltpu.VMEM
    dma = pltpu.SemaphoreType.DMA
    out = pl.pallas_call(
        kernel,
        out_shape=jax.ShapeDtypeStruct((2, WIDTH, 256), BF),
        in_specs=[
            pl.BlockSpec(memory_space=pltpu.VMEM),
            pl.BlockSpec(memory_space=pl.ANY),
            pl.BlockSpec(memory_space=pl.ANY),
        ],
        out_specs=pl.BlockSpec(memory_space=pltpu.VMEM),
        scratch_shapes=[
            vmem((HALF, 256), BF),
            vmem((AW, 256), BF),
            vmem((2, 4, 2 * BF_ROWS, 256), BF),
            vmem((2, 256), jnp.int32),
            vmem((2, 2 * WIDTH, 3584), BF),
            vmem((2, GROUPS, 8, 16, AW), BF),
            vmem((2, GROUPS, 8, 16, AW), BF),
            vmem((2, GROUPS, 4, 2, 16, AW), BF),
            vmem((2, GROUPS, 4, 16, AW), BF),
            vmem((2, GROUPS, 4, 2, 4, 16, AW), BF),
            vmem((GROUPS, 8, 16, BW), BF),
            vmem((GROUPS, 8, 16, BW), BF),
            vmem((GROUPS, 4, 2, 16, BW), BF),
            vmem((GROUPS, 4, 2, 16, BW), BF),
            vmem((2, 2 * WIDTH, 128), F32),
            vmem((2, GROUPS, 2, 4, 16, RET), BF),
            vmem((2, GROUPS, 4, 2, 16, RET), BF),
            vmem((2, GROUPS, 8, 16, RET), BF),
            vmem((GROUPS, 16, 16, RET), BF),
            vmem((GROUPS, 2, 128, 512), BF),
            vmem((GROUPS, 128, 512), BF),
            vmem((RET, 512), F32),
            dma((3,)),
            dma((3,)),
            dma((6,)),
            dma((2, units)),
            dma((4, units)),
            dma((8, units)),
            dma((8, units)),
            dma((2, GROUPS)),
            dma((2, GROUPS)),
            dma((2, 2, GROUPS)),
            dma((2, GROUPS)),
        ],
        compiler_params=pltpu.CompilerParams(
            collective_id=1, has_side_effects=True, vmem_limit_bytes=56 << 20
        ),
        cost_estimate=pl.CostEstimate(flops=3355443200, bytes_accessed=5000000, transcendentals=233472),
        name="routed_projections",
    )(ids, tok, w)
    return out.transpose(2, 0, 1)


def solution(mesh):
    return jax.shard_map(
        shards,
        mesh=mesh,
        in_specs=(P("expert", "tensor"), P("expert", None), P("expert", None, None, "tensor")),
        out_specs=P("expert", None, "tensor"),
        check_vma=False,
    )
```

time: 95.5 us -> 85.8 us (0.90)
  Pallas kernels: 93.7 us -> 83.9 us
    pallas_call x1, Pallas kernels: 93.7 us -> 83.9 us  [shards(): pl.pallas_call(kernel, out_shape=jax.ShapeDtypeStruct((2, WIDTH, 256), BF...]
where the time goes in v2:
time: 85.8 us; the launch traced here: 85.6 us
  Pallas kernels  83.9 us (98%)
  local copies, waits for them, and re-layouts  1.71 us (2%)
    pallas_call x1, Pallas kernels, shards(): pl.pallas_call(kernel, out_shape=jax.ShapeDtypeStruct((2, WIDTH, 256), BF...  83.9 us

profile of v2, /device:TPU:1, one launch (start us, length us, event | category | flops | bytes accessed | tf_op | source)
XLA Modules:
  0.0 85.6 jit_solution(8158054646820415920)
XLA Ops:
  0.0 83.9 %routed_projections.1 = bf16[2,304,256]{2,1,0:T(8,128)(2,1)} custom-call(s32[2,256]{1,0:T(2,128)} %bitcast.9, bf16[448,256]{1,0:T(8,128)(2,1)} %bitcast.8, bf16[608,3584]{1,0:T(8,128)(2,1)} %bitcast.7), custom_call_target="tpu_custom_call" | custom-call | flops 3355443200 | bytes 5000000 | tf_op jit(solution)/shard_map/routed_projections/pallas_call | solution.py:424
  83.9 1.7 %copy.5 = bf16[256,2,304]{0,2,1:T(8,128)(2,1)} copy(bf16[256,2,304]{0,2,1:T(8,128)(2,1)} %bitcast.6) | data formatting | bytes 622592

commit v3 on v2

--- a/solution.py
+++ b/solution.py
@@ -383,15 +383,15 @@
     stage_e(4)
     stage_eb(2)
     stage_r2(1)
-    stage_r4(0)
     stage_w(5)
     stage_f(5, 0)
     stage_h(2, 0)
     stage_f(5, 1)
     stage_h(2, 1)
-    stage_r4(1)
+    stage_r4(0)
     stage_k(2, 0)
     stage_k(2, 1)
+    stage_r4(1)
     stage_r4(2)
     for k in range(2):
         out_ref[k] = oacc[:WIDTH, k * 256 : (k + 1) * 256].astype(BF)
@@ -423,7 +423,7 @@
     dma = pltpu.SemaphoreType.DMA
     out = pl.pallas_call(
         kernel,
-        out_shape=jax.ShapeDtypeStruct((2, WIDTH, 256), BF),
+        out_shape=pltpu.VMEM((2, WIDTH, 256), BF),
         in_specs=[
             pl.BlockSpec(memory_space=pltpu.VMEM),
             pl.BlockSpec(memory_space=pl.ANY),

time: 85.8 us -> 82.4 us (0.960)
  Pallas kernels: 83.9 us -> 81.6 us
  local copies, waits for them, and re-layouts: 1.71 us -> 0.72 us
    pallas_call x1, Pallas kernels: 83.9 us -> 81.6 us  [shards(): pl.pallas_call(kernel, out_shape=pltpu.VMEM((2, WIDTH, 256), BF), in_spec...]
    unnamed x1, local copies, waits for them, and re-layouts: 1.71 us -> 0.72 us
where the time goes in v3:
time: 82.4 us; the launch traced here: 82.3 us
  Pallas kernels  81.6 us (99%)
    pallas_call x1, Pallas kernels, shards(): pl.pallas_call(kernel, out_shape=pltpu.VMEM((2, WIDTH, 256), BF), in_spec...  81.6 us

profile of v3, /device:TPU:1, one launch (start us, length us, event | category | flops | bytes accessed | tf_op | source)
XLA Modules:
  0.0 82.3 jit_solution(9793597432511130902)
XLA Ops:
  0.0 81.6 %routed_projections.1 = bf16[2,304,256]{2,1,0:T(8,128)(2,1)S(1)} custom-call(s32[2,256]{1,0:T(2,128)} %bitcast.9, bf16[448,256]{1,0:T(8,128)(2,1)} %bitcast.8, bf16[608,3584]{1,0:T(8,128)(2,1)} %bitcast.7), custom_call_target="tpu_custom_call" | custom-call | flops 3355443200 | bytes 5000000 | tf_op jit(solution)/shard_map/routed_projections/pallas_call | solution.py:424
  81.6 0.7 copy.5

commit v4 on v3

--- a/solution.py
+++ b/solution.py
@@ -357,27 +357,27 @@
     stage_ab(0)
     stage_m(1)
     stage_b(4)
-    stage_ab(1)
     w_local.wait()
     w_remote.wait()
     stage_e(0)
     stage_d(2)
     stage_c(4)
     stage_b(5)
-    stage_ab(2)
+    stage_ab(1)
     stage_bb(0)
     stage_e(1)
     stage_eb(0)
     stage_r1(0)
     stage_d(3)
     stage_c(5)
+    stage_ab(2)
     stage_bb(1)
     stage_e(2)
     stage_d(4)
-    stage_r2(0)
     stage_e(3)
     stage_eb(1)
     stage_r1(1)
+    stage_r2(0)
     stage_bb(2)
     stage_d(5)
     stage_e(4)

time: 82.4 us -> 82.5 us (level)
  no operation moved by 1% of the time
where the time goes in v4:
time: 82.5 us; the launch traced here: 82.3 us
  Pallas kernels  81.6 us (99%)
    pallas_call x1, Pallas kernels, shards(): pl.pallas_call(kernel, out_shape=pltpu.VMEM((2, WIDTH, 256), BF), in_spec...  81.6 us

profile of v4, /device:TPU:1, one launch (start us, length us, event | category | flops | bytes accessed | tf_op | source)
XLA Modules:
  0.0 82.3 jit_solution(1145372394718751066)
XLA Ops:
  0.0 81.6 %routed_projections.1 = bf16[2,304,256]{2,1,0:T(8,128)(2,1)S(1)} custom-call(s32[2,256]{1,0:T(2,128)} %bitcast.9, bf16[448,256]{1,0:T(8,128)(2,1)} %bitcast.8, bf16[608,3584]{1,0:T(8,128)(2,1)} %bitcast.7), custom_call_target="tpu_custom_call" | custom-call | flops 3355443200 | bytes 5000000 | tf_op jit(solution)/shard_map/routed_projections/pallas_call | solution.py:424
  81.6 0.7 copy.5
